TPU v7x, 512 devices: a whole 4x8x8 slice. The times are simulated.
512 devices in a mesh: rec: 16 (over z, core), frame: 32 (over x, y).
Axes of the slice: x: 4, y: 8, z: 8, core: 2. Of those that a mesh axis runs over, the one named last changes fastest.
Arguments:
- frames: bfloat16 [16, 49152, 256], P('rec', 'frame'), may hold values from -10 to 10
- texts: bfloat16 [32, 224, 256], P('rec', 'frame'), may hold values from -100 to 100
- pair_rec: int32 [32, 1], replicated, may hold values from 0 to 15, as said below
- pair_text: int32 [32], replicated, may hold values from 0 to 31, as said below
- pair_label: int32 [32], replicated, may hold values 0 or 1
Outputs:
- loss: float32 [], replicated
- grad_frames: bfloat16 [16, 49152, 256], P('rec', 'frame')
- grad_texts: bfloat16 [32, 224, 256], P('rec', 'frame')
Inputs may be any that keep to these rules, and one draw needn't show every extreme that they name: `pair_rec`: no recording is named by more than 6 pairs, some recording by exactly 6, and every recording by at least one. A pair's text is held by the index of rec one after, one before, or 8 after its recording (counted round): pair_text // 2 = (pair_rec + k) mod 16 with k one of 1, 15, 8.
All inputs are finite; a program needn't handle non-finite values.
Results may differ from a plain program's by a relative error of at most 0.0085.
Values may be sent and summed in bfloat16 or wider, within the bound.
A program may use at most 64 MiB of HBM per device.

v0:
```python
import jax
import jax.numpy as jnp
from jax import lax
from jax.sharding import PartitionSpec as P

MOST = 6
EPS = 1e-06
TEMP = 10.0
BIAS = -1.0
LOSS_SCALE = 2048.0


def slot_tables(pair_rec, pair_text, pair_label, here, most):
    record = pair_rec[:, 0]
    count = record.shape[0]
    order = jnp.arange(count, dtype=jnp.int32)
    same = (record[:, None] == record[None, :]).astype(jnp.int32)
    earlier = (order[None, :] < order[:, None]).astype(jnp.int32)
    rank = jnp.sum(same * earlier, axis=1)
    places = jnp.arange(most, dtype=jnp.int32)
    chosen = ((record[None, :] == here) & (rank[None, :] == places[:, None])).astype(jnp.int32)
    valid = jnp.sum(chosen, axis=1)
    slot_text = jnp.sum(chosen * pair_text[None, :], axis=1)
    sign = jnp.sum(chosen * (2 * pair_label[None, :] - 1), axis=1)
    return (valid, slot_text, sign)


def pair_terms(score, valid, sign, tokens):
    margin = -sign * (TEMP * score + BIAS)
    loss_part = valid * jax.nn.softplus(margin)
    grad_cos = -LOSS_SCALE * TEMP * valid * sign * jax.nn.sigmoid(margin) / tokens
    return (loss_part, grad_cos)


def body(frames, texts, pair_rec, pair_text, pair_label):
    here = lax.axis_index("rec")
    part = lax.axis_index("frame")
    owned, width_rows, width = texts.shape
    tokens = width_rows * lax.axis_size("frame")
    n_text = owned * lax.axis_size("rec")
    valid, slot_text, sign = slot_tables(pair_rec, pair_text, pair_label, here, MOST)
    valid_f = valid.astype(jnp.float32)
    sign_f = sign.astype(jnp.float32)
    picks = (
        (slot_text[:, None] == jnp.arange(n_text, dtype=jnp.int32)[None, :]) & (valid[:, None] > 0)
    ).astype(jnp.bfloat16)
    whole = lax.all_gather(texts, "frame", axis=1, tiled=True)
    query_vectors = jnp.einsum(
        "jc,cgx->jgx",
        picks,
        lax.all_gather(whole, "rec", axis=0, tiled=True),
        preferred_element_type=jnp.float32,
    ).astype(jnp.bfloat16)
    upstream_signal = frames[0]
    logit_scale = width ** (-0.5)
    pair_scores = (
        jnp.einsum(
            "ype,je->ypj", query_vectors, upstream_signal, preferred_element_type=jnp.float32
        )
        * logit_scale
    )
    local_max = jnp.max(pair_scores, axis=2)
    row_max = lax.pmax(local_max, "frame")
    expo = jnp.exp(pair_scores - row_max[..., None])
    batch_weights = expo.astype(jnp.bfloat16)
    value_partial = jnp.einsum(
        "pqx,xh->pqh", batch_weights, upstream_signal, preferred_element_type=jnp.float32
    )
    query_f = query_vectors.astype(jnp.float32)
    q_norm = lax.rsqrt(jnp.sum(query_f * query_f, axis=2) + EPS)
    q_unit = query_f * q_norm[..., None]
    context = lax.psum(value_partial, "frame")
    c_norm = lax.rsqrt(jnp.sum(context * context, axis=2) + EPS)
    c_unit = context * c_norm[..., None]
    cos = jnp.sum(q_unit * c_unit, axis=2)
    score = jnp.mean(cos, axis=1)
    loss_part, grad_cos = pair_terms(score, valid_f, sign_f, tokens)
    weight = grad_cos[:, None, None]
    d_context = weight * (q_unit - cos[..., None] * c_unit) * c_norm[..., None]
    direct = weight * (c_unit - cos[..., None] * q_unit) * q_norm[..., None]
    direct_own = lax.dynamic_slice_in_dim(direct, part * width_rows, width_rows, 1)
    context_batch_gradient = d_context.astype(jnp.bfloat16)
    weight_gradient = jnp.einsum(
        "ype,je->ypj", context_batch_gradient, upstream_signal, preferred_element_type=jnp.float32
    )
    score_gradient = (expo * weight_gradient * logit_scale).astype(jnp.bfloat16)
    d_query = lax.psum_scatter(
        jnp.einsum(
            "slf,fd->lsd", score_gradient, upstream_signal, preferred_element_type=jnp.float32
        ),
        "frame",
        scatter_dimension=0,
        tiled=True,
    )
    d_query = d_query + jnp.transpose(direct_own, (1, 0, 2))
    text_term = jnp.einsum(
        "st,lsd->tld", picks.astype(jnp.float32), d_query, precision=lax.Precision.HIGHEST
    )
    grad_texts = lax.psum_scatter(text_term, "rec", scatter_dimension=0, tiled=True).astype(
        jnp.bfloat16
    )
    frame_loss_piece = jnp.einsum(
        "cvm,cvz->mz", score_gradient, query_vectors, preferred_element_type=jnp.float32
    )
    frame_loss_piece = frame_loss_piece + jnp.einsum(
        "cvm,cvz->mz", batch_weights, context_batch_gradient, preferred_element_type=jnp.float32
    )
    grad_frames = frame_loss_piece.astype(jnp.bfloat16)[None]
    loss = lax.psum(jnp.sum(loss_part), "rec")
    return (loss, grad_frames, grad_texts)


def solution(mesh):
    return jax.shard_map(
        body,
        mesh=mesh,
        in_specs=(P("rec", "frame", None), P("rec", "frame", None), P(), P(), P()),
        out_specs=(P(), P("rec", "frame", None), P("rec", "frame", None)),
        check_vma=False,
    )
```

profile of v0, /device:TPU:16, one launch (start us, length us, event | category | flops | bytes accessed | tf_op | source)
XLA Modules:
  0.0 644.4 jit_solution(15901261809968272552)
XLA Ops:
  7.2 49.8 %all_gather.6 = bf16[2,224,256]{2,0,1:T(2,128)(2,1)S(1)} all-gather(bf16[2,7,256]{2,0,1:T(2,128)(2,1)} %param.6), channel_id=1, replica_groups=mesh['rec'=16,'frame'=32] {'frame'}, dimensions={1}, use_global_device_ids=true | all-gather | bytes 236544 | tf_op jit(solution)/shard_map/all_gather | solution.py:47
  57.0 0.7 copy.20
  57.8 0.9 select_reduce_fusion
  58.7 0.7 broadcast_compare_fusion.1
  59.4 0.7 multiply_add_fusion
  60.1 1.3 select_reduce_fusion.2
  61.4 43.4 %all-gather.2.cloned.1.call-done = bf16[32,224,256]{2,1,0:T(8,128)(2,1)} async-done(((bf16[2,224,256]{2,1,0:T(8,128)(2,1)}), bf16[32,224,256]{2,1,0:T(8,128)(2,1)}) %all-gather.2.cloned.1.call-update) | async-done | bytes 3670032 | tf_op jit(solution)/shard_map/all_gather | solution.py:51
  104.7 4.3 fusion.6
  109.0 4.4 multiply_reduce_fusion
  113.4 71.4 %pmax.7 = f32[6,224]{1,0:T(8,128)S(1)} all-reduce(f32[6,224]{1,0:T(8,128)S(1)} %get-tuple-element.17), channel_id=1, replica_groups=mesh['rec'=16,'frame'=32] {'frame'}, use_global_device_ids=true, to_apply=%region_6.0 | all-reduce | flops 1344 | bytes 10752 | tf_op jit(solution)/shard_map/pmax | solution.py:63
  184.8 4.9 fusion.13
  189.7 2.1 copy.23
  191.8 0.2 reduce-scatter.3.cloned.1.call-start
  192.0 0.7 add_rsqrt_fusion.1
  192.6 157.1 %all-reduce.5.cloned.1.call-done = f32[6,224,256]{2,0,1:T(8,128)} async-done(((f32[6,224,256]{2,0,1:T(8,128)}), f32[6,224,256]{2,0,1:T(8,128)}) %all-reduce.5.cloned.1.call-update) | async-done | bytes 1376272 | tf_op jit(solution)/shard_map/psum | solution.py:72
  349.7 1.9 multiply_reduce_fusion.1
  351.6 2.4 multiply_reduce_fusion.2
  354.0 1.4 fusion.44
  355.4 1.8 convert_multiply_fusion
  357.2 4.9 multiply_convert_fusion
  362.2 1.3 fusion.10
  363.5 0.7 copy-done.10
  364.2 2.1 copy.47
  366.2 1.3 dynamic-slice
  368.2 0.7 constant_dynamic-slice_fusion
  368.9 0.7 constant_dynamic-slice_fusion.1
  369.6 5.7 convolution_bitcast_fusion
  375.3 2.3 fusion.5
  377.6 209.2 %reduce-scatter.3.cloned.1.call-done = f32[7,6,256]{2,1,0:T(8,128)} async-done(((f32[224,6,256]{2,1,0:T(8,128)}), f32[7,6,256]{2,1,0:T(8,128)}) %reduce-scatter.3.cloned.1.call-update) | async-done | bytes 43024 | tf_op jit(solution)/shard_map/reduce_scatter | solution.py:87
  586.9 1.3 fusion.27
  588.2 49.1 %all-reduce.6 = (f32[]{:T(128)}, bf16[32,7,256]{2,0,1:T(8,128)(2,1)S(1)}) all-reduce(f32[]{:T(128)} %get-tuple-element.14, f32[32,7,256]{2,0,1:T(8,128)S(1)} %fusion.27), channel_id=1, replica_groups=mesh['rec'=16,'frame'=32] {'rec'}, use_global_device_ids=true, to_apply=%region_11.12 | all-reduce | flops 57345 | bytes 344072 | tf_op jit(solution)/shard_map/psum | solution.py:109
  637.3 0.6 dynamic-slice_convert_fusion
  (30 shorter events, 0.2 us)
Async XLA Ops:
  7.2 101.8 %copy-start = (bf16[1,1536,256]{2,1,0:T(8,128)(2,1)S(1)}, bf16[1,1536,256]{2,1,0:T(8,128)(2,1)}, u32[]{:S(2)}) copy-start(bf16[1,1536,256]{2,1,0:T(8,128)(2,1)} %param.5) | copy-start | bytes 2359300
  7.2 97.5 %all-gather.2.cloned.1.call-start = ((), (), s32[]{:S(2)}) async-start(), calls=%async_computation.1 | async-start | bytes 3899392 | tf_op jit(solution)/shard_map/all_gather | solution.py:51
  57.8 291.9 %all-reduce.5.cloned.1.call-start = ((), (), s32[]{:S(2)}) async-start(), calls=%async_computation.2 | async-start | bytes 3670016 | tf_op jit(solution)/shard_map/psum | solution.py:72
  61.3 43.4 %copy-start.9 = (s32[6]{0:T(128)}, s32[6]{0:T(128)S(1)}, u32[]{:S(2)}) copy-start(s32[6]{0:T(128)S(1)} %get-tuple-element.7) | copy-start | bytes 76
  61.3 47.6 %copy-start.4 = (s32[6]{0:T(128)}, s32[6]{0:T(128)S(1)}, u32[]{:S(2)}) copy-start(s32[6]{0:T(128)S(1)} %get-tuple-element.6) | copy-start | bytes 76
  61.4 47.6 %copy-start.8 = (pred[6]{0:T(512)(128)(4,1)}, pred[6]{0:T(512)(128)(4,1)S(1)}, u32[]{:S(2)}) copy-start(pred[6]{0:T(512)(128)(4,1)S(1)} %broadcast_compare_fusion) | copy-start | bytes 22
  191.8 395.1 %reduce-scatter.3.cloned.1.call-start = ((), (), s32[]{:S(2)}) async-start(), calls=%async_computation.3 | async-start | bytes 1892352 | tf_op jit(solution)/shard_map/reduce_scatter | solution.py:87
  349.7 5.7 copy-start.1
  354.0 3.2 copy-start.3
  355.4 6.8 %copy-start.6 = (f32[6]{0:T(128)}, f32[6]{0:T(128)S(1)}, u32[]{:S(2)}) copy-start(f32[6]{0:T(128)S(1)} %get-tuple-element.13) | copy-start | bytes 76
  357.2 5.0 copy-start.2
  362.2 2.0 copy-start.10
  369.6 5.7 copy-start.11
  375.3 211.6 %copy-start.5 = (s32[6]{0:T(128)S(1)}, s32[6]{0:T(128)}, u32[]{:S(2)}) copy-start(s32[6]{0:T(128)} %copy-done.4) | copy-start | bytes 76
  375.3 211.6 %copy-start.7 = (f32[6]{0:T(128)S(1)}, f32[6]{0:T(128)}, u32[]{:S(2)}) copy-start(f32[6]{0:T(128)} %copy-done.6) | copy-start | bytes 76
Sparse Core Ops, SparseCore 0:
  57.9 46.7 all-gather.1
  191.9 157.7 all-reduce.4
  366.4 220.4 reduce-scatter.2
where the time goes:
time: 645 us; the launch traced here: 644 us
  waiting for transfers between devices  410 us (64%)
  blocking collectives  170 us (26%)
  matrix products  29 us (4%)
  between operations  14.6 us (2%)
  other arithmetic  11.7 us (2%)
  local copies, waits for them, and re-layouts  8.88 us (1%)
    reduce_scatter x1, waiting for transfers between devices, body(): lax.psum_scatter(jnp.einsum('slf,fd->lsd', score_gradient, upstream_signa...  209 us
    psum x1, waiting for transfers between devices, body(): context = lax.psum(value_partial, 'frame')  157 us
    pmax x1, blocking collectives, body(): row_max = lax.pmax(local_max, 'frame')  71.4 us
    all_gather x1, blocking collectives, body(): whole = lax.all_gather(texts, 'frame', axis=1, tiled=True)  49.8 us
    psum x1, blocking collectives, body(): loss = lax.psum(jnp.sum(loss_part), 'rec')  49.1 us
    all_gather x1, waiting for transfers between devices, body(): lax.all_gather(whole, 'rec', axis=0, tiled=True)  43.4 us
  transfers between devices with their start and end apart: 3, of which 3 were waited for; matrix products, arithmetic and copies ran while one was open for 2% of the time, Pallas kernels for 0%

commit v1 on v0

--- a/solution.py
+++ b/solution.py
@@ -8,6 +8,19 @@
 TEMP = 10.0
 BIAS = -1.0
 LOSS_SCALE = 2048.0
+
+
+def ring_gather(array, axis, dim):
+    ways = lax.axis_size(axis)
+    up = [(d, (d + 1) % ways) for d in range(ways)]
+    down = [(d, (d - 1) % ways) for d in range(ways)]
+    earlier, later = ([array], [array])
+    for _ in range(ways // 2):
+        earlier.append(lax.ppermute(earlier[-1], axis, up))
+    for _ in range((ways - 1) // 2):
+        later.append(lax.ppermute(later[-1], axis, down))
+    line = jnp.concatenate([*earlier[::-1], *later[1:]], axis=dim)
+    return jnp.roll(line, (lax.axis_index(axis) - ways // 2) * array.shape[dim], axis=dim)
 
 
 def slot_tables(pair_rec, pair_text, pair_label, here, most):
@@ -46,10 +59,7 @@
     ).astype(jnp.bfloat16)
     whole = lax.all_gather(texts, "frame", axis=1, tiled=True)
     query_vectors = jnp.einsum(
-        "jc,cgx->jgx",
-        picks,
-        lax.all_gather(whole, "rec", axis=0, tiled=True),
-        preferred_element_type=jnp.float32,
+        "jc,cgx->jgx", picks, ring_gather(whole, "rec", 0), preferred_element_type=jnp.float32
     ).astype(jnp.bfloat16)
     upstream_signal = frames[0]
     logit_scale = width ** (-0.5)

time: 645 us -> 691 us (1.071)
  local copies, waits for them, and re-layouts: 8.88 us -> 42.4 us
  starting transfers between devices: 0.3 us -> 22.1 us
  waiting for transfers between devices: 410 us -> 400 us
    all_gather x1 -> x0, waiting for transfers between devices: 43.4 us -> none  [body(): lax.all_gather(whole, 'rec', axis=0, tiled=True)]
    concatenate x0 -> x1, local copies, waits for them, and re-layouts: none -> 34.3 us  [ring_gather(): jnp.roll(line, (lax.axis_index(axis) - ways // 2) * array.shape[dim], axi...]
    ppermute x0 -> x15, waiting for transfers between devices: none -> 28.8 us  [the longest x8 28.5 us: ring_gather(): earlier.append(lax.ppermute(earlier[-1], axis, up))]
    ppermute x0 -> x15, starting transfers between devices: none -> 21.8 us  [the longest x7 21.8 us: ring_gather(): later.append(lax.ppermute(later[-1], axis, down))]
  transfers between devices with their start and end apart: 3 -> 17, of which waited for: 3 -> 11; matrix products, arithmetic and copies ran while one was open for 2% -> 2% of each run, Pallas kernels for 0% -> 0%
where the time goes in v1:
time: 691 us; the launch traced here: 688 us
  waiting for transfers between devices  400 us (58%)
  blocking collectives  169 us (24%)
  local copies, waits for them, and re-layouts  42.4 us (6%)
  matrix products  28.4 us (4%)
  starting transfers between devices  22.1 us (3%)
  between operations  14.9 us (2%)
  other arithmetic  11.7 us (2%)
    reduce_scatter x1, waiting for transfers between devices, body(): lax.psum_scatter(jnp.einsum('slf,fd->lsd', score_gradient, upstream_signa...  209 us
    psum x1, waiting for transfers between devices, body(): context = lax.psum(value_partial, 'frame')  161 us
    pmax x1, blocking collectives, body(): row_max = lax.pmax(local_max, 'frame')  70.5 us
    all_gather x1, blocking collectives, body(): whole = lax.all_gather(texts, 'frame', axis=1, tiled=True)  49.8 us
    psum x1, blocking collectives, body(): loss = lax.psum(jnp.sum(loss_part), 'rec')  49.1 us
    concatenate x1, local copies, waits for them, and re-layouts, ring_gather(): jnp.roll(line, (lax.axis_index(axis) - ways // 2) * array.shape[dim], axi...  34.3 us
    ppermute x8, waiting for transfers between devices, ring_gather(): earlier.append(lax.ppermute(earlier[-1], axis, up))  28.5 us
    ppermute x7, starting transfers between devices, ring_gather(): later.append(lax.ppermute(later[-1], axis, down))  21.8 us
  transfers between devices with their start and end apart: 17, of which 11 were waited for; matrix products, arithmetic and copies ran while one was open for 2% of the time, Pallas kernels for 0%

profile of v1, /device:TPU:16, one launch (start us, length us, event | category | flops | bytes accessed | tf_op | source)
XLA Modules:
  0.0 688.4 jit_solution(10468660774895816834)
XLA Ops:
  7.2 49.8 %all_gather.3 = bf16[2,224,256]{2,0,1:T(2,128)(2,1)S(1)} all-gather(bf16[2,7,256]{2,0,1:T(2,128)(2,1)} %param.6), channel_id=1, replica_groups=mesh['rec'=16,'frame'=32] {'frame'}, dimensions={1}, use_global_device_ids=true | all-gather | bytes 236544 | tf_op jit(solution)/shard_map/all_gather | solution.py:60
  57.0 2.9 collective-permute-start.8
  60.0 3.7 collective-permute-done
  63.7 3.6 collective-permute-start.9
  67.3 3.5 collective-permute-done.1
  70.9 3.1 collective-permute-start.10
  74.0 3.5 collective-permute-done.2
  77.5 3.1 collective-permute-start.11
  80.6 3.5 collective-permute-done.3
  84.2 3.1 collective-permute-start.12
  87.3 3.5 collective-permute-done.4
  91.5 3.0 collective-permute-start.13
  94.5 3.0 collective-permute-done.5
  99.1 3.0 collective-permute-start.14
  102.0 2.2 collective-permute-done.6
  105.9 5.3 collective-permute-done.7
  111.2 34.3 %concatenate.6 = bf16[64,224,256]{2,0,1:T(8,128)(2,1)} concatenate(bf16[2,224,256]{2,0,1:T(2,128)(2,1)} %collective-permute-done.7, bf16[2,224,256]{2,0,1:T(2,128)(2,1)} %collective-permute-done.6, bf16[2,224,256]{2,0,1:T(2,128)(2,1)S(1)} %collective-permute-done.5, bf16[2,224,256]{2,0,1:T(2,128)(2,1)S(1)} %collective-permute-done.4, ...), dimensions={0} | concatenate | bytes 14680064 | tf_op jit(solution)/shard_map/jit(_roll_dynamic)/concatenate | solution.py:23
  145.5 3.6 fusion.6
  149.1 4.5 multiply_reduce_fusion
  153.6 70.5 %pmax.7 = f32[6,224]{1,0:T(8,128)S(1)} all-reduce(f32[6,224]{1,0:T(8,128)S(1)} %get-tuple-element.17), channel_id=1, replica_groups=mesh['rec'=16,'frame'=32] {'frame'}, use_global_device_ids=true, to_apply=%region_6.7 | all-reduce | flops 1344 | bytes 10752 | tf_op jit(solution)/shard_map/pmax | solution.py:73
  224.1 4.9 fusion.13
  229.0 2.1 copy.19
  231.9 161.3 %all-reduce.5.cloned.1.call-done = f32[6,224,256]{2,0,1:T(8,128)} async-done(((f32[6,224,256]{2,0,1:T(8,128)}), f32[6,224,256]{2,0,1:T(8,128)}) %all-reduce.5.cloned.1.call-update) | async-done | bytes 1376272 | tf_op jit(solution)/shard_map/psum | solution.py:82
  393.2 1.9 multiply_reduce_fusion.1
  395.1 2.4 multiply_reduce_fusion.2
  398.9 1.8 convert_multiply_fusion
  400.7 4.9 multiply_convert_fusion
  407.7 2.1 copy.37
  413.1 5.7 convolution_bitcast_fusion
  418.8 2.3 fusion.5
  421.1 209.4 %reduce-scatter.3.cloned.1.call-done = f32[7,6,256]{2,1,0:T(8,128)} async-done(((f32[224,6,256]{2,1,0:T(8,128)}), f32[7,6,256]{2,1,0:T(8,128)}) %reduce-scatter.3.cloned.1.call-update) | async-done | bytes 43024 | tf_op jit(solution)/shard_map/reduce_scatter | solution.py:97
  631.8 49.1 %all-reduce.6 = (f32[]{:T(128)}, bf16[32,7,256]{2,0,1:T(8,128)(2,1)S(1)}) all-reduce(f32[]{:T(128)} %get-tuple-element.14, f32[32,7,256]{2,0,1:T(8,128)S(1)} %fusion.27), channel_id=1, replica_groups=mesh['rec'=16,'frame'=32] {'rec'}, use_global_device_ids=true, to_apply=%region_11.12 | all-reduce | flops 57345 | bytes 344072 | tf_op jit(solution)/shard_map/psum | solution.py:119
  (57 shorter events, 12.8 us)
Async XLA Ops:
  7.2 142.0 %copy-start = (bf16[1,1536,256]{2,1,0:T(8,128)(2,1)S(1)}, bf16[1,1536,256]{2,1,0:T(8,128)(2,1)}, u32[]{:S(2)}) copy-start(bf16[1,1536,256]{2,1,0:T(8,128)(2,1)} %param.5) | copy-start | bytes 2359300
  7.2 386.0 %all-reduce.5.cloned.1.call-start = ((), (), s32[]{:S(2)}) async-start(), calls=%async_computation.1 | async-start | bytes 3670016 | tf_op jit(solution)/shard_map/psum | solution.py:82
  57.0 6.7 collective-permute-start
  57.0 6.6 collective-permute-start.8
  63.7 7.2 %collective-permute-start.1 = (bf16[2,224,256]{2,0,1:T(2,128)(2,1)S(1)}, bf16[2,224,256]{2,0,1:T(2,128)(2,1)S(1)}, u32[]{:S(2)}, u32[]{:S(2)}) collective-permute-start(bf16[2,224,256]{2,0,1:T(2,128)(2,1)S(1)} %collective-permute-done), channel_id=1, source_target_pairs={{0,32},{32,64},{64,96},{96,128},{128,160},{160,192},{192,224},{224... | collective-permute-start | bytes 688136 | tf_op jit(solution)/shard_map/ppermute | solution.py:19
  63.7 7.2 %collective-permute-start.9 = (bf16[2,224,256]{2,0,1:T(2,128)(2,1)S(1)}, bf16[2,224,256]{2,0,1:T(2,128)(2,1)S(1)}, u32[]{:S(2)}, u32[]{:S(2)}) collective-permute-start(bf16[2,224,256]{2,0,1:T(2,128)(2,1)S(1)} %collective-permute-done.8), channel_id=1, source_target_pairs={{0,480},{32,0},{64,32},{96,64},{128,96},{160,128},{192,160},{224,1... | collective-permute-start | bytes 688136 | tf_op jit(solution)/shard_map/ppermute | solution.py:21
  70.9 6.7 collective-permute-start.2
  70.9 6.7 collective-permute-start.10
  77.5 6.7 collective-permute-start.3
  77.5 6.7 collective-permute-start.11
  84.2 6.7 collective-permute-start.4
  84.2 7.3 %collective-permute-start.12 = (bf16[2,224,256]{2,0,1:T(2,128)(2,1)S(1)}, bf16[2,224,256]{2,0,1:T(2,128)(2,1)S(1)}, u32[]{:S(2)}, u32[]{:S(2)}) collective-permute-start(bf16[2,224,256]{2,0,1:T(2,128)(2,1)S(1)} %collective-permute-done.11), channel_id=1, source_target_pairs={{0,480},{32,0},{64,32},{96,64},{128,96},{160,128},{192,160},{224,1... | collective-permute-start | bytes 688136 | tf_op jit(solution)/shard_map/ppermute | solution.py:21
  90.8 6.7 collective-permute-start.5
  91.5 7.6 %collective-permute-start.13 = (bf16[2,224,256]{2,0,1:T(2,128)(2,1)S(1)}, bf16[2,224,256]{2,0,1:T(2,128)(2,1)}, u32[]{:S(2)}, u32[]{:S(2)}) collective-permute-start(bf16[2,224,256]{2,0,1:T(2,128)(2,1)S(1)} %collective-permute-done.12), channel_id=1, source_target_pairs={{0,480},{32,0},{64,32},{96,64},{128,96},{160,128},{192,160},{224,1... | collective-permute-start | bytes 688136 | tf_op jit(solution)/shard_map/ppermute | solution.py:21
  97.5 6.8 collective-permute-start.6
  99.1 6.8 collective-permute-start.14
  104.3 7.0 %collective-permute-start.7 = (bf16[2,224,256]{2,0,1:T(2,128)(2,1)}, bf16[2,224,256]{2,0,1:T(2,128)(2,1)}, u32[]{:S(2)}, u32[]{:S(2)}) collective-permute-start(bf16[2,224,256]{2,0,1:T(2,128)(2,1)} %collective-permute-done.6), channel_id=1, source_target_pairs={{0,32},{32,64},{64,96},{96,128},{128,160},{160,192},{192,224},{224... | collective-permute-start | bytes 688136 | tf_op jit(solution)/shard_map/ppermute | solution.py:19
  105.6 40.0 %copy-start.8 = (s32[6]{0:T(128)}, s32[6]{0:T(128)S(1)}, u32[]{:S(2)}) copy-start(s32[6]{0:T(128)S(1)} %get-tuple-element.7) | copy-start | bytes 76
  105.6 40.0 %copy-start.6 = (s32[6]{0:T(128)}, s32[6]{0:T(128)S(1)}, u32[]{:S(2)}) copy-start(s32[6]{0:T(128)S(1)} %get-tuple-element.6) | copy-start | bytes 76
  105.6 40.0 %copy-start.9 = (pred[6]{0:T(512)(128)(4,1)}, pred[6]{0:T(512)(128)(4,1)S(1)}, u32[]{:S(2)}) copy-start(pred[6]{0:T(512)(128)(4,1)S(1)} %broadcast_compare_fusion) | copy-start | bytes 22
  231.0 399.5 %reduce-scatter.3.cloned.1.call-start = ((), (), s32[]{:S(2)}) async-start(), calls=%async_computation.2 | async-start | bytes 1892352 | tf_op jit(solution)/shard_map/reduce_scatter | solution.py:97
  393.2 5.7 copy-start.1
  397.5 3.2 copy-start.3
  398.9 6.8 copy-start.4
  400.7 5.0 copy-start.2
  405.7 2.0 copy-start.10
  413.1 5.7 copy-start.11
  418.8 211.8 %copy-start.5 = (f32[6]{0:T(128)S(1)}, f32[6]{0:T(128)}, u32[]{:S(2)}) copy-start(f32[6]{0:T(128)} %copy-done.4) | copy-start | bytes 76
  418.8 211.8 %copy-start.7 = (s32[6]{0:T(128)S(1)}, s32[6]{0:T(128)}, u32[]{:S(2)}) copy-start(s32[6]{0:T(128)} %copy-done.6) | copy-start | bytes 76
Sparse Core Ops, SparseCore 0:
  231.2 162.0 all-reduce.4
  409.9 220.6 reduce-scatter.2
